TPU v7x, 128 devices: a whole 4x4x4 slice. The times are simulated.
128 devices in a mesh: clus: 128 (over x, z, y, core).
Axes of the slice: x: 4, y: 4, z: 4, core: 2. Of those that a mesh axis runs over, the one named last changes fastest.
Arguments:
- features: bfloat16 [262144, 128], P('clus'), may hold values from -6 to 6
- basis_t: bfloat16 [1024, 64, 256], P('clus'), may hold values from -0.375 to 0.375
- send_list: int32 [128, 128, 1], P('clus'), may hold values from 0 to 7
- couple_rows: int32 [49152], P('clus'), may hold values from 0 to 7
- couple_cols: int32 [49152], P('clus'), may hold values from 0 to 127, as said below
- couple_blocks: bfloat16 [49152, 4096], P('clus'), may hold values from -0.078125 to 0.078125
- near_rows: int32 [8192], P('clus'), may hold values from 0 to 7
- near_cols: int32 [8192], P('clus'), may hold values from 0 to 11
- near_blocks: bfloat16 [8192, 256, 256], P('clus'), may hold values from -0.09375 to 0.09375
Outputs:
- product: bfloat16 [262144, 128], P('clus')
Inputs may be any that keep to these rules, and one draw needn't show every extreme that they name: Slot s of the slots that device p fills for device q holds local leaf send_list[p, q, s] of device p. `couple_cols`: on device d, slot p + s is the slot that device p fills for d with index s.
All inputs are finite; a program needn't handle non-finite values.
Results may differ from a plain program's by a relative error of at most 0.013.
Values may be sent and summed in bfloat16 or wider, within the bound.
A program may use at most 128 MiB of HBM per device.

v0:
```python
import functools

import jax
import jax.numpy as jnp
from jax import lax
from jax.experimental import pallas as pl
from jax.experimental.pallas import tpu as pltpu
from jax.sharding import PartitionSpec as P

HALO = 2
MESH = pl.DeviceIdType.MESH
F32 = jnp.float32
BF16 = jnp.bfloat16


def chain(keys, count):
    n = keys.shape[0]
    at = jnp.arange(n, dtype=jnp.int32)
    same = (keys[:, None] == keys[None, :]) & (at[None, :] < at[:, None])
    prev = jnp.max(jnp.where(same, at[None, :], -1), axis=1)
    ids = jnp.arange(count, dtype=jnp.int32)
    last = jnp.max(jnp.where(ids[:, None] == keys[None, :], at[None, :], -1), axis=1)
    return jnp.where(prev < 0, n, prev), jnp.where(last < 0, n, last)


def kernel(
    n,
    leaves,
    rank,
    leaf,
    rhs,
    cb,
    nb,
    send_ref,
    cprev_ref,
    clast_ref,
    nrows_ref,
    ncols_ref,
    rprev_ref,
    rlast_ref,
    kprev_ref,
    klast_ref,
    qprev_ref,
    qlast_ref,
    x_hbm,
    basis_hbm,
    blocks_hbm,
    near_hbm,
    out_hbm,
    xext,
    basis,
    basis_t,
    blocks,
    near,
    coef,
    coef_f,
    coef_t,
    x_t,
    outgoing,
    received,
    plain,
    rolled,
    dense,
    sums,
    back,
    total,
    raw,
    chained,
    work,
    back_sum,
    near_sum,
    rim_out,
    rim_in,
    out,
    far_f,
    load_sem,
    send1,
    recv1,
    send2,
    recv2,
    hsend,
    hrecv,
    rsend,
    rrecv,
):
    me = lax.axis_index("clus")
    half = rank // 2
    lane = lax.broadcasted_iota(jnp.int32, (rank, 2 * rank), 1)
    low = lane < rank
    low_half = lax.broadcasted_iota(jnp.int32, (half, 2 * rank), 1) < rank

    barrier = pltpu.get_barrier_semaphore()

    load_x = pltpu.make_async_copy(x_hbm, xext.at[pl.ds(HALO, leaves)], load_sem.at[0])
    load_b = pltpu.make_async_copy(basis_hbm, basis, load_sem.at[1])
    load_s = pltpu.make_async_copy(blocks_hbm, blocks, load_sem.at[2])
    load_n = pltpu.make_async_copy(near_hbm, near, load_sem.at[3])
    load_x.start()
    load_b.start()
    load_s.start()
    load_n.start()

    def greet(i, carry):
        q = lax.rem(me + i, n)
        pl.semaphore_signal(barrier, inc=1, device_id=(q,), device_id_type=MESH)
        return carry

    lax.fori_loop(1, n, greet, 0)

    load_x.wait()
    load_b.wait()

    def coefficients(g, carry):
        c = jnp.dot(basis[g], xext[HALO + g], preferred_element_type=F32).astype(BF16)
        coef[g] = c
        coef_f[g] = c.astype(F32)
        return carry

    lax.fori_loop(0, leaves, coefficients, 0)

    pl.semaphore_wait(barrier, n - 1)

    def forward_copy(q):
        return pltpu.make_async_remote_copy(
            src_ref=outgoing.at[q],
            dst_ref=received.at[pl.ds(pl.multiple_of(me * rank, rank), rank)],
            send_sem=send1.at[q],
            recv_sem=recv1.at[me],
            device_id=(q,),
            device_id_type=MESH,
        )

    def send_coef(i, carry):
        q = lax.rem(me + i, n)
        outgoing[q] = coef[send_ref[q]]
        forward_copy(q).start()
        return carry

    lax.fori_loop(1, n, send_coef, 0)
    received[pl.ds(pl.multiple_of(me * rank, rank), rank), :] = coef[send_ref[me]]

    to_next = pltpu.make_async_remote_copy(
        src_ref=xext.at[pl.ds(leaves, HALO)],
        dst_ref=xext.at[pl.ds(0, HALO)],
        send_sem=hsend.at[0],
        recv_sem=hrecv.at[0],
        device_id=(lax.rem(me + 1, n),),
        device_id_type=MESH,
    )
    to_prior = pltpu.make_async_remote_copy(
        src_ref=xext.at[pl.ds(HALO, HALO)],
        dst_ref=xext.at[pl.ds(HALO + leaves, HALO)],
        send_sem=hsend.at[1],
        recv_sem=hrecv.at[1],
        device_id=(lax.rem(me + n - 1, n),),
        device_id_type=MESH,
    )
    has_next = me < n - 1
    has_prior = me > 0

    @pl.when(has_next)
    def _():
        to_next.start()

    @pl.when(has_prior)
    def _():
        to_prior.start()

    @pl.when(jnp.logical_not(has_prior))
    def _():
        xext[0:HALO] = jnp.zeros((HALO, leaf, rhs), BF16)

    @pl.when(jnp.logical_not(has_next))
    def _():
        xext[HALO + leaves :] = jnp.zeros((HALO, leaf, rhs), BF16)

    for pair in range(leaves // 2):
        rows = []
        for g in (2 * pair, 2 * pair + 1):
            for odd in range(2):
                rows.append(coef_f[g, pl.ds(odd, half, stride=2), :])
        tile = jnp.concatenate(rows, axis=0)
        coef_t[:, pair * 2 * rank : (pair + 1) * 2 * rank] = tile.T.astype(BF16)

    load_s.wait()

    chained[cb] = jnp.zeros((half, 2 * rank), F32)
    plain[cb] = jnp.zeros((half, 2 * rank), BF16)
    rolled[cb] = jnp.zeros((half, 2 * rank), BF16)

    def spread(t, carry):
        for j in range(half):
            piece = blocks[pl.ds(pl.multiple_of(t * 16, 16), 16), j * 2 * rank : (j + 1) * 2 * rank]
            raw[pl.ds(j, 16, stride=half), :] = piece.astype(F32)
        for s in range(16):
            k = t * 16 + s
            value = raw[s * half : (s + 1) * half, :] + chained[cprev_ref[k]]
            chained[k] = value
            plain[k] = value.astype(BF16)
            rolled[k] = pltpu.roll(value, rank, 1).astype(BF16)
        return carry

    lax.fori_loop(0, cb // 16, spread, 0)

    groups = n // 4
    my_group = me // 4

    def back_copy(q):
        return pltpu.make_async_remote_copy(
            src_ref=sums.at[q],
            dst_ref=back.at[me],
            send_sem=send2.at[q],
            recv_sem=recv2.at[me],
            device_id=(q,),
            device_id_type=MESH,
        )

    def mirror(i, carry):
        g = lax.rem(my_group + i, groups)
        for pair in range(2):
            for r in range(leaves):
                k0 = clast_ref[(g * 4 + 2 * pair) * leaves + r]
                k1 = clast_ref[(g * 4 + 2 * pair + 1) * leaves + r]
                upper = jnp.where(low_half, plain[k0], rolled[k1])
                lower = jnp.where(low_half, rolled[k0], plain[k1])
                cols = pl.ds(pair * 2 * rank, 2 * rank)
                dense[g, r * rank : r * rank + half, cols] = upper
                dense[g, r * rank + half : (r + 1) * rank, cols] = lower
        product = jnp.dot(coef_t[...], dense[g], preferred_element_type=F32)
        for pair in range(2):
            part = product[:, pair * 2 * rank : (pair + 1) * 2 * rank]
            top, bottom = part[:rank], part[rank:]
            turned = pltpu.roll(jnp.where(low, bottom, top), rank, 1)
            sums[g * 4 + 2 * pair] = jnp.where(low, top, turned).astype(BF16)
            sums[g * 4 + 2 * pair + 1] = jnp.where(low, turned, bottom).astype(BF16)
        for s in range(4):
            q = g * 4 + s

            @pl.when(q != me)
            def _():
                back_copy(q).start()

            @pl.when(q == me)
            def _():
                back[me] = sums[me]

        return carry

    lax.fori_loop(0, groups, mirror, 0)

    for g in range(leaves):
        x_t[g] = xext[HALO + g].astype(F32).T.astype(BF16)
        basis_t[g] = basis[g].astype(F32).T.astype(BF16)

    @pl.when(has_prior)
    def _():
        to_next.wait_recv()

    @pl.when(has_next)
    def _():
        to_prior.wait_recv()

    load_n.wait()
    work[nb] = jnp.zeros((leaf, rhs), F32)

    def near_rows(k, carry):
        y = jnp.dot(near[k], xext[ncols_ref[k]], preferred_element_type=F32)
        work[k] = y + work[rprev_ref[k]]
        return carry

    lax.fori_loop(0, nb, near_rows, 0)
    for g in range(leaves):
        near_sum[g] = work[rlast_ref[g]]

    def near_cols(k, carry):
        y = jnp.dot(x_t[nrows_ref[k]], near[k], preferred_element_type=F32)
        before = work[kprev_ref[k]]
        for h in range(2):
            rows = slice(h * rhs, (h + 1) * rhs)
            work[k, rows, :] = y[:, rows] + before[rows]
        return carry

    lax.fori_loop(0, nb, near_cols, 0)

    def spread_of(c):
        return work[klast_ref[c]]

    for h in range(HALO):
        rim_out[0, h] = spread_of(h).astype(BF16)
        rim_out[1, h] = spread_of(HALO + leaves + h).astype(BF16)
    rim_prior = pltpu.make_async_remote_copy(
        src_ref=rim_out.at[0],
        dst_ref=rim_in.at[0],
        send_sem=rsend.at[0],
        recv_sem=rrecv.at[0],
        device_id=(lax.rem(me + n - 1, n),),
        device_id_type=MESH,
    )
    rim_next = pltpu.make_async_remote_copy(
        src_ref=rim_out.at[1],
        dst_ref=rim_in.at[1],
        send_sem=rsend.at[1],
        recv_sem=rrecv.at[1],
        device_id=(lax.rem(me + 1, n),),
        device_id_type=MESH,
    )

    @pl.when(has_prior)
    def _():
        rim_prior.start()

    @pl.when(has_next)
    def _():
        rim_next.start()

    def add_turned(g, y):
        for h in range(2):
            rows = slice(h * rhs, (h + 1) * rhs)
            near_sum[g, rows, :] += y[rows].T

    for g in range(leaves):
        add_turned(g, spread_of(HALO + g))

    total[...] = jnp.zeros_like(total)
    step = min(4, groups)

    def forward(i, carry):
        for s in range(4 * step):
            q = i * 4 * step + s

            @pl.when(q != me)
            def _():
                pltpu.make_async_remote_copy(
                    src_ref=outgoing.at[q],
                    dst_ref=received.at[pl.ds(pl.multiple_of(q * rank, rank), rank)],
                    send_sem=send1.at[q],
                    recv_sem=recv1.at[q],
                    device_id=(q,),
                    device_id_type=MESH,
                ).wait_recv()

        acc = total[...]
        for s in range(step):
            g = i * step + s
            c = received[pl.ds(pl.multiple_of(g * 4 * rank, 4 * rank), 4 * rank), :]
            acc = acc + jnp.dot(dense[g], c, preferred_element_type=F32)
        total[...] = acc
        return carry

    lax.fori_loop(0, groups // step, forward, 0)

    @pl.when(has_next)
    def _():
        rim_prior.wait_recv()
        for h in range(HALO):
            add_turned(leaves - HALO + h, rim_in[0, h].astype(F32))

    @pl.when(has_prior)
    def _():
        rim_next.wait_recv()
        for h in range(HALO):
            add_turned(h, rim_in[1, h].astype(F32))

    back_sum[n] = jnp.zeros((rank, rhs), F32)

    def returned(q, carry):
        @pl.when(q != me)
        def _():
            pltpu.make_async_remote_copy(
                src_ref=sums.at[q],
                dst_ref=back.at[q],
                send_sem=send2.at[q],
                recv_sem=recv2.at[q],
                device_id=(q,),
                device_id_type=MESH,
            ).wait_recv()

        back_sum[q] = back[q].astype(F32) + back_sum[qprev_ref[q]]
        return carry

    lax.fori_loop(0, n, returned, 0)

    for g in range(leaves):
        y = back_sum[qlast_ref[g]]
        turned = jnp.concatenate([y, pltpu.roll(y, rank, 1)], axis=0).T
        far_f[g, pl.ds(0, half, stride=2), :] = total[g * rank : g * rank + half, :]
        far_f[g, pl.ds(1, half, stride=2), :] = total[g * rank + half : (g + 1) * rank, :]
        far = (far_f[g] + turned[:rank]).astype(BF16)
        down = jnp.dot(basis_t[g], far, preferred_element_type=F32)
        out[g * leaf : (g + 1) * leaf, :] = (down + near_sum[g]).astype(BF16)

    store = pltpu.make_async_copy(out, out_hbm, load_sem.at[0])
    store.start()

    def drain(i, carry):
        q = lax.rem(me + i, n)
        forward_copy(q).wait_send()
        back_copy(q).wait_send()
        return carry

    lax.fori_loop(1, n, drain, 0)

    @pl.when(has_next)
    def _():
        to_next.wait_send()
        rim_next.wait_send()

    @pl.when(has_prior)
    def _():
        to_prior.wait_send()
        rim_prior.wait_send()

    store.wait()


def per_device(
    features,
    basis_t,
    send_list,
    couple_rows,
    couple_cols,
    couple_blocks,
    near_rows,
    near_cols,
    near_blocks,
):
    n = lax.axis_size("clus")
    leaves, rank, leaf = basis_t.shape
    rhs = features.shape[1]
    cb, nb = couple_blocks.shape[0], near_blocks.shape[0]
    send = send_list.reshape(-1)
    cprev, clast = chain(couple_cols * leaves + couple_rows, n * leaves)
    rprev, rlast = chain(near_rows, leaves)
    kprev, klast = chain(near_cols, leaves + 2 * HALO)
    qprev, qlast = chain(send, leaves)
    half = rank // 2
    wide = leaves + 2 * HALO
    dma = pltpu.SemaphoreType.DMA
    smem = pl.BlockSpec(memory_space=pltpu.SMEM)
    anywhere = pl.BlockSpec(memory_space=pl.ANY)
    return pl.pallas_call(
        functools.partial(kernel, n, leaves, rank, leaf, rhs, cb, nb),
        out_shape=jax.ShapeDtypeStruct(features.shape, BF16),
        in_specs=[smem] * 11 + [anywhere] * 4,
        out_specs=anywhere,
        scratch_shapes=[
            pltpu.VMEM((wide, leaf, rhs), BF16),
            pltpu.VMEM((leaves, rank, leaf), BF16),
            pltpu.VMEM((leaves, leaf, rank), BF16),
            pltpu.VMEM(couple_blocks.shape, BF16),
            pltpu.VMEM(near_blocks.shape, BF16),
            pltpu.VMEM((leaves, rank, rhs), BF16),
            pltpu.VMEM((leaves, rank, rhs), F32),
            pltpu.VMEM((rhs, leaves * rank), BF16),
            pltpu.VMEM((leaves, rhs, leaf), BF16),
            pltpu.VMEM((n, rank, rhs), BF16),
            pltpu.VMEM((n * rank, rhs), BF16),
            pltpu.VMEM((cb + 1, half, 2 * rank), BF16),
            pltpu.VMEM((cb + 1, half, 2 * rank), BF16),
            pltpu.VMEM((n // 4, leaves * rank, 4 * rank), BF16),
            pltpu.VMEM((n, rank, rhs), BF16),
            pltpu.VMEM((n, rank, rhs), BF16),
            pltpu.VMEM((leaves * rank, rhs), F32),
            pltpu.VMEM((16 * half, 2 * rank), F32),
            pltpu.VMEM((cb + 1, half, 2 * rank), F32),
            pltpu.VMEM((nb + 1, leaf, rhs), F32),
            pltpu.VMEM((n + 1, rank, rhs), F32),
            pltpu.VMEM((leaves, leaf, rhs), F32),
            pltpu.VMEM((2, HALO, leaf, rhs), BF16),
            pltpu.VMEM((2, HALO, leaf, rhs), BF16),
            pltpu.VMEM((leaves * leaf, rhs), BF16),
            pltpu.VMEM((leaves, rank, rhs), F32),
            dma((4,)),
            dma((n,)),
            dma((n,)),
            dma((n,)),
            dma((n,)),
            dma((2,)),
            dma((2,)),
            dma((2,)),
            dma((2,)),
        ],
        compiler_params=pltpu.CompilerParams(
            collective_id=0, has_side_effects=True, vmem_limit_bytes=60 * 1024 * 1024
        ),
    )(
        send,
        cprev,
        clast,
        near_rows,
        near_cols,
        rprev,
        rlast,
        kprev,
        klast,
        qprev,
        qlast,
        features.reshape(leaves, leaf, rhs),
        basis_t,
        couple_blocks,
        near_blocks,
    )


def solution(mesh):
    placed = (
        P("clus", None),
        P("clus", None, None),
        P("clus", None, None),
        P("clus"),
        P("clus"),
        P("clus", None),
        P("clus"),
        P("clus"),
        P("clus", None, None),
    )
    return jax.shard_map(
        per_device, mesh=mesh, in_specs=placed, out_specs=P("clus", None), check_vma=False
    )
```

profile of v0, /device:TPU:34, one launch (start us, length us, event | category | flops | bytes accessed | tf_op | source)
XLA Modules:
  0.0 116.1 jit_solution(5899066048428096335)
XLA Ops:
  0.0 0.8 select_reduce_fusion.6
  0.8 0.9 select_reduce_fusion.2
  1.7 0.6 compare_select_fusion.3.qprev_ref
  2.3 0.9 select_reduce_fusion.4
  3.2 0.8 select_reduce_fusion.7
  4.0 0.5 compare_select_fusion.2
  4.5 0.9 select_reduce_fusion.3
  5.4 0.6 compare_select_fusion.5
  6.0 0.8 select_reduce_fusion.5
  6.8 0.6 compare_select_fusion.4.klast_ref
  7.4 0.7 multiply_add_fusion
  8.1 0.2 select_reduce_fusion.1
  8.3 0.6 compare_select_fusion.1.cprev_ref
  8.9 0.3 select_reduce_fusion
  9.2 0.6 compare_select_fusion.clast_ref
  9.8 104.5 %shard_map.91 = bf16[2048,128]{1,0:T(8,128)(2,1)} custom-call(s32[128]{0:T(128)} %bitcast.5, s32[384]{0:T(512)} %compare_select_fusion.1.cprev_ref, s32[1024]{0:T(1024)} %compare_select_fusion.clast_ref, s32[64]{0:T(128)} %nrows_ref.1, s32[64]{0:T(128)} %ncols_ref.1, s32[64]{0:T(128)} %get-tuple-element.8.rprev_ref, s32[8]{0:T(128)} %get-tuple-element.6.rlast_ref, ...), custom_call_target="tpu_custom_call" | custom-call | tf_op jit(solution)/shard_map/pallas_call | solution.py:441
  114.3 1.9 %copy.11 = bf16[2048,128]{1,0:T(8,128)(2,1)} copy(bf16[2048,128]{1,0:T(8,128)(2,1)} %shard_map.91) | data formatting | bytes 1048576
where the time goes:
time: 116 us
  Pallas kernels  104 us (90%)
  other arithmetic  9.78 us (8%)
  local copies, waits for them, and re-layouts  1.87 us (2%)
    pallas_call x1, Pallas kernels, per_device(): pl.pallas_call(functools.partial(kernel, n, leaves, rank, leaf, rhs, cb,...  104 us
    select_n x6, other arithmetic, chain(): return (jnp.where(prev < 0, n, prev), jnp.where(last < 0, n, last))  3.5 us
    reduce_max x4, other arithmetic, chain(): prev = jnp.max(jnp.where(same, at[None, :], -1), axis=1)  2.97 us
    reduce_max x4, other arithmetic, chain(): jnp.max(jnp.where(ids[:, None] == keys[None, :], at[None, :], -1), axis=1)  2.61 us

commit v1 on v0

--- a/solution.py
+++ b/solution.py
@@ -1,7 +1,9 @@
 import functools
+import random
 
 import jax
 import jax.numpy as jnp
+import numpy as np
 from jax import lax
 from jax.experimental import pallas as pl
 from jax.experimental.pallas import tpu as pltpu
@@ -13,14 +15,31 @@
 BF16 = jnp.bfloat16
 
 
-def chain(keys, count):
-    n = keys.shape[0]
-    at = jnp.arange(n, dtype=jnp.int32)
+def chains(parts):
+    keys, first, size = [], [], []
+    seen, length = 0, 0
+    for part, count in parts:
+        keys.append(part + seen)
+        first.append(np.stack([np.full(part.shape[0], length), np.full(part.shape[0], part.shape[0])]))
+        size.append(np.stack([np.full(count, length), np.full(count, part.shape[0])]))
+        seen, length = seen + count, length + part.shape[0]
+    keys = jnp.concatenate(keys)
+    at = jnp.arange(length, dtype=jnp.int32)
+    ids = jnp.arange(seen, dtype=jnp.int32)
     same = (keys[:, None] == keys[None, :]) & (at[None, :] < at[:, None])
     prev = jnp.max(jnp.where(same, at[None, :], -1), axis=1)
-    ids = jnp.arange(count, dtype=jnp.int32)
     last = jnp.max(jnp.where(ids[:, None] == keys[None, :], at[None, :], -1), axis=1)
-    return jnp.where(prev < 0, n, prev), jnp.where(last < 0, n, last)
+    first, size = (np.concatenate(v, axis=1).astype(np.int32) for v in (first, size))
+    prev = jnp.where(prev < 0, first[1], prev - first[0])
+    last = jnp.where(last < 0, size[1], last - size[0])
+    return prev, last
+
+
+def far_first(n):
+    steps = [(o // 32, o // 8 % 4, o // 2 % 4, o % 2) for o in range(1, n)]
+    random.Random(0).shuffle(steps)
+    steps.sort(key=lambda o: -sum(min(v, 4 - v) for v in o[:3]))
+    return steps
 
 
 def kernel(
@@ -32,16 +51,10 @@
     cb,
     nb,
     send_ref,
-    cprev_ref,
-    clast_ref,
     nrows_ref,
     ncols_ref,
-    rprev_ref,
-    rlast_ref,
-    kprev_ref,
-    klast_ref,
-    qprev_ref,
-    qlast_ref,
+    prev_ref,
+    last_ref,
     x_hbm,
     basis_hbm,
     blocks_hbm,
@@ -84,6 +97,9 @@
     rrecv,
 ):
     me = lax.axis_index("clus")
+    cprev, rprev, kprev, qprev = 0, cb, cb + nb, cb + 2 * nb
+    clast, rlast = 0, n * leaves
+    klast, qlast = rlast + leaves, rlast + 2 * leaves + 2 * HALO
     half = rank // 2
     lane = lax.broadcasted_iota(jnp.int32, (rank, 2 * rank), 1)
     low = lane < rank
@@ -130,13 +146,15 @@
             device_id_type=MESH,
         )
 
-    def send_coef(i, carry):
-        q = lax.rem(me + i, n)
+    def peer(step):
+        x, z, y, core = me // 32, me // 8 % 4, me // 2 % 4, me % 2
+        dx, dz, dy, dc = step
+        return (((x + dx) % (n // 32) * 4 + (z + dz) % 4) * 4 + (y + dy) % 4) * 2 + (core + dc) % 2
+
+    for step in far_first(n):
+        q = peer(step)
         outgoing[q] = coef[send_ref[q]]
         forward_copy(q).start()
-        return carry
-
-    lax.fori_loop(1, n, send_coef, 0)
     received[pl.ds(pl.multiple_of(me * rank, rank), rank), :] = coef[send_ref[me]]
 
     to_next = pltpu.make_async_remote_copy(
@@ -194,13 +212,13 @@
             raw[pl.ds(j, 16, stride=half), :] = piece.astype(F32)
         for s in range(16):
             k = t * 16 + s
-            value = raw[s * half : (s + 1) * half, :] + chained[cprev_ref[k]]
+            value = raw[s * half : (s + 1) * half, :] + chained[prev_ref[cprev + k]]
             chained[k] = value
             plain[k] = value.astype(BF16)
             rolled[k] = pltpu.roll(value, rank, 1).astype(BF16)
         return carry
 
-    lax.fori_loop(0, cb // 16, spread, 0)
+    lax.fori_loop(0, cb // 16, spread, 0, unroll=1)
 
     groups = n // 4
     my_group = me // 4
@@ -216,17 +234,20 @@
         )
 
     def mirror(i, carry):
-        g = lax.rem(my_group + i, groups)
-        for pair in range(2):
-            for r in range(leaves):
-                k0 = clast_ref[(g * 4 + 2 * pair) * leaves + r]
-                k1 = clast_ref[(g * 4 + 2 * pair + 1) * leaves + r]
-                upper = jnp.where(low_half, plain[k0], rolled[k1])
-                lower = jnp.where(low_half, rolled[k0], plain[k1])
-                cols = pl.ds(pair * 2 * rank, 2 * rank)
-                dense[g, r * rank : r * rank + half, cols] = upper
-                dense[g, r * rank + half : (r + 1) * rank, cols] = lower
-        product = jnp.dot(coef_t[...], dense[g], preferred_element_type=F32)
+        g = lax.rem(my_group + i * 13, groups)
+        rows = []
+        for r in range(leaves):
+            upper, lower = [], []
+            for pair in range(2):
+                k0 = last_ref[clast + (g * 4 + 2 * pair) * leaves + r]
+                k1 = last_ref[clast + (g * 4 + 2 * pair + 1) * leaves + r]
+                upper.append(jnp.where(low_half, plain[k0], rolled[k1]))
+                lower.append(jnp.where(low_half, rolled[k0], plain[k1]))
+            rows.append(jnp.concatenate(upper, axis=1))
+            rows.append(jnp.concatenate(lower, axis=1))
+        tile = jnp.concatenate(rows, axis=0)
+        dense[g] = tile
+        product = jnp.dot(coef_t[...], tile, preferred_element_type=F32)
         for pair in range(2):
             part = product[:, pair * 2 * rank : (pair + 1) * 2 * rank]
             top, bottom = part[:rank], part[rank:]
@@ -246,7 +267,7 @@
 
         return carry
 
-    lax.fori_loop(0, groups, mirror, 0)
+    lax.fori_loop(0, groups, mirror, 0, unroll=2)
 
     for g in range(leaves):
         x_t[g] = xext[HALO + g].astype(F32).T.astype(BF16)
@@ -265,25 +286,25 @@
 
     def near_rows(k, carry):
         y = jnp.dot(near[k], xext[ncols_ref[k]], preferred_element_type=F32)
-        work[k] = y + work[rprev_ref[k]]
-        return carry
-
-    lax.fori_loop(0, nb, near_rows, 0)
+        work[k] = y + work[prev_ref[rprev + k]]
+        return carry
+
+    lax.fori_loop(0, nb, near_rows, 0, unroll=8)
     for g in range(leaves):
-        near_sum[g] = work[rlast_ref[g]]
+        near_sum[g] = work[last_ref[rlast + g]]
 
     def near_cols(k, carry):
         y = jnp.dot(x_t[nrows_ref[k]], near[k], preferred_element_type=F32)
-        before = work[kprev_ref[k]]
+        before = work[prev_ref[kprev + k]]
         for h in range(2):
             rows = slice(h * rhs, (h + 1) * rhs)
             work[k, rows, :] = y[:, rows] + before[rows]
         return carry
 
-    lax.fori_loop(0, nb, near_cols, 0)
+    lax.fori_loop(0, nb, near_cols, 0, unroll=8)
 
     def spread_of(c):
-        return work[klast_ref[c]]
+        return work[last_ref[klast + c]]
 
     for h in range(HALO):
         rim_out[0, h] = spread_of(h).astype(BF16)
@@ -375,13 +396,13 @@
                 device_id_type=MESH,
             ).wait_recv()
 
-        back_sum[q] = back[q].astype(F32) + back_sum[qprev_ref[q]]
-        return carry
-
-    lax.fori_loop(0, n, returned, 0)
+        back_sum[q] = back[q].astype(F32) + back_sum[prev_ref[qprev + q]]
+        return carry
+
+    lax.fori_loop(0, n, returned, 0, unroll=4)
 
     for g in range(leaves):
-        y = back_sum[qlast_ref[g]]
+        y = back_sum[last_ref[qlast + g]]
         turned = jnp.concatenate([y, pltpu.roll(y, rank, 1)], axis=0).T
         far_f[g, pl.ds(0, half, stride=2), :] = total[g * rank : g * rank + half, :]
         far_f[g, pl.ds(1, half, stride=2), :] = total[g * rank + half : (g + 1) * rank, :]
@@ -429,10 +450,14 @@
     rhs = features.shape[1]
     cb, nb = couple_blocks.shape[0], near_blocks.shape[0]
     send = send_list.reshape(-1)
-    cprev, clast = chain(couple_cols * leaves + couple_rows, n * leaves)
-    rprev, rlast = chain(near_rows, leaves)
-    kprev, klast = chain(near_cols, leaves + 2 * HALO)
-    qprev, qlast = chain(send, leaves)
+    prev, last = chains(
+        [
+            (couple_cols * leaves + couple_rows, n * leaves),
+            (near_rows, leaves),
+            (near_cols, leaves + 2 * HALO),
+            (send, leaves),
+        ]
+    )
     half = rank // 2
     wide = leaves + 2 * HALO
     dma = pltpu.SemaphoreType.DMA
@@ -441,7 +466,7 @@
     return pl.pallas_call(
         functools.partial(kernel, n, leaves, rank, leaf, rhs, cb, nb),
         out_shape=jax.ShapeDtypeStruct(features.shape, BF16),
-        in_specs=[smem] * 11 + [anywhere] * 4,
+        in_specs=[smem] * 5 + [anywhere] * 4,
         out_specs=anywhere,
         scratch_shapes=[
             pltpu.VMEM((wide, leaf, rhs), BF16),
@@ -485,16 +510,10 @@
         ),
     )(
         send,
-        cprev,
-        clast,
         near_rows,
         near_cols,
-        rprev,
-        rlast,
-        kprev,
-        klast,
-        qprev,
-        qlast,
+        prev,
+        last,
         features.reshape(leaves, leaf, rhs),
         basis_t,
         couple_blocks,

time: 116 us -> 84 us (0.72)
  the two profiles are of different devices: /device:TPU:34 before, /device:TPU:98 now
where the time goes in v1:
time: 84 us; the launch traced here: 83.7 us
  Pallas kernels  76.2 us (91%)
  other arithmetic  5.6 us (7%)
  local copies, waits for them, and re-layouts  1.87 us (2%)
    pallas_call x1, Pallas kernels, per_device(): pl.pallas_call(functools.partial(kernel, n, leaves, rank, leaf, rhs, cb,...  76.2 us
    unnamed x1, local copies, waits for them, and re-layouts  1.87 us

profile of v1, /device:TPU:98, one launch (start us, length us, event | category | flops | bytes accessed | tf_op | source)
XLA Modules:
  0.0 83.7 jit_solution(5901267855306255508)
XLA Ops:
  0.0 0.7 broadcast_add_fusion
  0.7 0.7 broadcast_add_fusion.1
  1.3 0.7 multiply_add_fusion
  2.0 0.1 pad_add_fusion
  2.1 0.4 select_reduce_fusion.1
  2.5 1.3 %add_select_fusion.1.prev_ref = s32[640]{0:T(1024)} fusion(s32[640]{0:T(1024)} %constant.24.clone, s32[640]{0:T(1024)S(1)} %select_reduce_fusion.1, s32[640]{0:T(1024)} %constant.32), kind=kLoop, calls=%fused_computation.7 | loop fusion | flops 1920 | bytes 10240 | tf_op jit(solution)/shard_map/jit(_where)/select_n | solution.py:33
  3.8 0.5 select_reduce_fusion
  4.3 1.3 %add_select_fusion.last_ref = s32[1052]{0:T(1024)} fusion(s32[1052]{0:T(1024)} %constant.26.clone, s32[1052]{0:T(1024)S(1)} %select_reduce_fusion, s32[1052]{0:T(1024)} %constant.33), kind=kLoop, calls=%fused_computation.5 | loop fusion | flops 3156 | bytes 16832 | tf_op jit(solution)/shard_map/jit(_where)/select_n | solution.py:34
  5.6 76.2 %shard_map.127 = bf16[2048,128]{1,0:T(8,128)(2,1)} custom-call(s32[128]{0:T(128)} %bitcast.4, s32[64]{0:T(128)} %nrows_ref.1, s32[64]{0:T(128)} %ncols_ref.1, s32[640]{0:T(1024)} %add_select_fusion.1.prev_ref, s32[1052]{0:T(1024)} %add_select_fusion.last_ref, bf16[8,256,128]{2,1,0:T(8,128)(2,1)} %bitcast.3, bf16[8,64,256]{2,1,0:T(8,128)(2,1)} %basis_hbm.1, ...), custom_call_target="tpu_custom_call" | custom-call | tf_op jit(solution)/shard_map/pallas_call | solution.py:466
  81.8 1.9 %copy.15 = bf16[2048,128]{1,0:T(8,128)(2,1)} copy(bf16[2048,128]{1,0:T(8,128)(2,1)} %shard_map.127) | data formatting | bytes 1048576

commit v2 on v1

--- a/solution.py
+++ b/solution.py
@@ -3,7 +3,6 @@
 
 import jax
 import jax.numpy as jnp
-import numpy as np
 from jax import lax
 from jax.experimental import pallas as pl
 from jax.experimental.pallas import tpu as pltpu
@@ -15,30 +14,42 @@
 BF16 = jnp.bfloat16
 
 
-def chains(parts):
-    keys, first, size = [], [], []
-    seen, length = 0, 0
-    for part, count in parts:
-        keys.append(part + seen)
-        first.append(np.stack([np.full(part.shape[0], length), np.full(part.shape[0], part.shape[0])]))
-        size.append(np.stack([np.full(count, length), np.full(count, part.shape[0])]))
-        seen, length = seen + count, length + part.shape[0]
-    keys = jnp.concatenate(keys)
-    at = jnp.arange(length, dtype=jnp.int32)
-    ids = jnp.arange(seen, dtype=jnp.int32)
-    same = (keys[:, None] == keys[None, :]) & (at[None, :] < at[:, None])
-    prev = jnp.max(jnp.where(same, at[None, :], -1), axis=1)
-    last = jnp.max(jnp.where(ids[:, None] == keys[None, :], at[None, :], -1), axis=1)
-    first, size = (np.concatenate(v, axis=1).astype(np.int32) for v in (first, size))
-    prev = jnp.where(prev < 0, first[1], prev - first[0])
-    last = jnp.where(last < 0, size[1], last - size[0])
-    return prev, last
-
-
-def far_first(n):
+def chains(keys_ref, prev_ref, last_ref, parts, id_parts):
+    blocks = keys_ref.shape[0]
+    row = lax.broadcasted_iota(jnp.int32, (128, 128), 0)
+    col = lax.broadcasted_iota(jnp.int32, (128, 128), 1)
+    down = [jnp.broadcast_to(keys_ref[b : b + 1, :], (128, 128)).T for b in range(blocks)]
+    lane = lax.broadcasted_iota(jnp.int32, (1, 128), 1)
+
+    def settle(found, place, bounds):
+        start, length = jnp.zeros_like(place), jnp.zeros_like(place)
+        for first, (at, size) in bounds:
+            start = jnp.where(place >= first, at, start)
+            length = jnp.where(place >= first, size, length)
+        return jnp.where(found < 0, length, jnp.clip(found - start, 0, length))
+
+    for b in range(blocks):
+        key = keys_ref[b : b + 1, :]
+        best = jnp.full((128, 128), -1, jnp.int32)
+        for other in range(b + 1):
+            hit = down[other] == key
+            if other == b:
+                hit = hit & (row < col)
+            best = jnp.where(hit, row + other * 128, best)
+        found = jnp.max(best, axis=0, keepdims=True)
+        prev_ref[b : b + 1, :] = settle(found, lane + b * 128, [(start, (start, size)) for start, size in parts])
+    for b in range(last_ref.shape[0]):
+        best = jnp.full((128, 128), -1, jnp.int32)
+        for other in range(blocks):
+            best = jnp.where(down[other] == lane + b * 128, row + other * 128, best)
+        found = jnp.max(best, axis=0, keepdims=True)
+        last_ref[b : b + 1, :] = settle(found, lane + b * 128, [(first, parts[part]) for first, part in id_parts])
+
+
+def near_first(n):
     steps = [(o // 32, o // 8 % 4, o // 2 % 4, o % 2) for o in range(1, n)]
     random.Random(0).shuffle(steps)
-    steps.sort(key=lambda o: -sum(min(v, 4 - v) for v in o[:3]))
+    steps.sort(key=lambda o: sum(min(v, 4 - v) for v in o[:3]))
     return steps
 
 
@@ -50,11 +61,8 @@
     rhs,
     cb,
     nb,
-    send_ref,
-    nrows_ref,
-    ncols_ref,
-    prev_ref,
-    last_ref,
+    key_ref,
+    keys,
     x_hbm,
     basis_hbm,
     blocks_hbm,
@@ -86,6 +94,10 @@
     rim_in,
     out,
     far_f,
+    prev_v,
+    last_v,
+    prev_s,
+    last_s,
     load_sem,
     send1,
     recv1,
@@ -97,9 +109,18 @@
     rrecv,
 ):
     me = lax.axis_index("clus")
-    cprev, rprev, kprev, qprev = 0, cb, cb + nb, cb + 2 * nb
-    clast, rlast = 0, n * leaves
-    klast, qlast = rlast + leaves, rlast + 2 * leaves + 2 * HALO
+    base = last_v.shape[0] * 128 - 128
+    rprev, kprev, qprev = cb, cb + nb, cb + 2 * nb
+    rlast, klast, qlast = base, base + leaves, base + 2 * leaves + 2 * HALO
+    parts = [(0, cb), (rprev, nb), (kprev, nb), (qprev, n)]
+    id_parts = [(0, 0), (rlast, 1), (klast, 2), (qlast, 3)]
+
+    def at(ref, i):
+        return ref[i // 128, i % 128]
+
+    def target(q):
+        return jnp.maximum(at(key_ref, qprev + q) - qlast, 0)
+
     half = rank // 2
     lane = lax.broadcasted_iota(jnp.int32, (rank, 2 * rank), 1)
     low = lane < rank
@@ -114,7 +135,6 @@
     load_x.start()
     load_b.start()
     load_s.start()
-    load_n.start()
 
     def greet(i, carry):
         q = lax.rem(me + i, n)
@@ -132,7 +152,8 @@
         coef_f[g] = c.astype(F32)
         return carry
 
-    lax.fori_loop(0, leaves, coefficients, 0)
+    lax.fori_loop(0, leaves, coefficients, 0, unroll=leaves)
+    load_n.start()
 
     pl.semaphore_wait(barrier, n - 1)
 
@@ -140,8 +161,8 @@
         return pltpu.make_async_remote_copy(
             src_ref=outgoing.at[q],
             dst_ref=received.at[pl.ds(pl.multiple_of(me * rank, rank), rank)],
-            send_sem=send1.at[q],
-            recv_sem=recv1.at[me],
+            send_sem=send1,
+            recv_sem=recv1,
             device_id=(q,),
             device_id_type=MESH,
         )
@@ -151,11 +172,11 @@
         dx, dz, dy, dc = step
         return (((x + dx) % (n // 32) * 4 + (z + dz) % 4) * 4 + (y + dy) % 4) * 2 + (core + dc) % 2
 
-    for step in far_first(n):
+    for step in near_first(n):
         q = peer(step)
-        outgoing[q] = coef[send_ref[q]]
+        outgoing[q] = coef[target(q)]
         forward_copy(q).start()
-    received[pl.ds(pl.multiple_of(me * rank, rank), rank), :] = coef[send_ref[me]]
+    received[pl.ds(pl.multiple_of(me * rank, rank), rank), :] = coef[target(me)]
 
     to_next = pltpu.make_async_remote_copy(
         src_ref=xext.at[pl.ds(leaves, HALO)],
@@ -200,6 +221,14 @@
         tile = jnp.concatenate(rows, axis=0)
         coef_t[:, pair * 2 * rank : (pair + 1) * 2 * rank] = tile.T.astype(BF16)
 
+    chains(keys, prev_v, last_v, parts, id_parts)
+    prev_load = pltpu.make_async_copy(prev_v, prev_s, load_sem.at[4])
+    last_load = pltpu.make_async_copy(last_v, last_s, load_sem.at[5])
+    prev_load.start()
+    last_load.start()
+    prev_load.wait()
+    last_load.wait()
+
     load_s.wait()
 
     chained[cb] = jnp.zeros((half, 2 * rank), F32)
@@ -212,7 +241,7 @@
             raw[pl.ds(j, 16, stride=half), :] = piece.astype(F32)
         for s in range(16):
             k = t * 16 + s
-            value = raw[s * half : (s + 1) * half, :] + chained[prev_ref[cprev + k]]
+            value = raw[s * half : (s + 1) * half, :] + chained[at(prev_s, k)]
             chained[k] = value
             plain[k] = value.astype(BF16)
             rolled[k] = pltpu.roll(value, rank, 1).astype(BF16)
@@ -222,13 +251,14 @@
 
     groups = n // 4
     my_group = me // 4
+    part = min(16, n // 2)
 
     def back_copy(q):
         return pltpu.make_async_remote_copy(
             src_ref=sums.at[q],
             dst_ref=back.at[me],
-            send_sem=send2.at[q],
-            recv_sem=recv2.at[me],
+            send_sem=send2,
+            recv_sem=recv2.at[me // part],
             device_id=(q,),
             device_id_type=MESH,
         )
@@ -239,8 +269,8 @@
         for r in range(leaves):
             upper, lower = [], []
             for pair in range(2):
-                k0 = last_ref[clast + (g * 4 + 2 * pair) * leaves + r]
-                k1 = last_ref[clast + (g * 4 + 2 * pair + 1) * leaves + r]
+                k0 = last_s[g // 4, g % 4 * 4 * leaves + 2 * pair * leaves + r]
+                k1 = last_s[g // 4, g % 4 * 4 * leaves + (2 * pair + 1) * leaves + r]
                 upper.append(jnp.where(low_half, plain[k0], rolled[k1]))
                 lower.append(jnp.where(low_half, rolled[k0], plain[k1]))
             rows.append(jnp.concatenate(upper, axis=1))
@@ -285,17 +315,17 @@
     work[nb] = jnp.zeros((leaf, rhs), F32)
 
     def near_rows(k, carry):
-        y = jnp.dot(near[k], xext[ncols_ref[k]], preferred_element_type=F32)
-        work[k] = y + work[prev_ref[rprev + k]]
+        y = jnp.dot(near[k], xext[jnp.maximum(at(key_ref, kprev + k) - klast, 0)], preferred_element_type=F32)
+        work[k] = y + work[at(prev_s, rprev + k)]
         return carry
 
     lax.fori_loop(0, nb, near_rows, 0, unroll=8)
     for g in range(leaves):
-        near_sum[g] = work[last_ref[rlast + g]]
+        near_sum[g] = work[at(last_s, rlast + g)]
 
     def near_cols(k, carry):
-        y = jnp.dot(x_t[nrows_ref[k]], near[k], preferred_element_type=F32)
-        before = work[prev_ref[kprev + k]]
+        y = jnp.dot(x_t[jnp.maximum(at(key_ref, rprev + k) - rlast, 0)], near[k], preferred_element_type=F32)
+        before = work[at(prev_s, kprev + k)]
         for h in range(2):
             rows = slice(h * rhs, (h + 1) * rhs)
             work[k, rows, :] = y[:, rows] + before[rows]
@@ -304,7 +334,7 @@
     lax.fori_loop(0, nb, near_cols, 0, unroll=8)
 
     def spread_of(c):
-        return work[last_ref[klast + c]]
+        return work[at(last_s, klast + c)]
 
     for h in range(HALO):
         rim_out[0, h] = spread_of(h).astype(BF16)
@@ -342,24 +372,21 @@
     for g in range(leaves):
         add_turned(g, spread_of(HALO + g))
 
+    others = pl.ds(0, (n - 1) * rank)
+    all_forward = pltpu.make_async_remote_copy(
+        src_ref=received.at[others],
+        dst_ref=received.at[others],
+        send_sem=send1,
+        recv_sem=recv1,
+        device_id=(lax.rem(me + 1, n),),
+        device_id_type=MESH,
+    )
+    all_forward.wait_recv()
+    all_forward.wait_send()
     total[...] = jnp.zeros_like(total)
     step = min(4, groups)
 
     def forward(i, carry):
-        for s in range(4 * step):
-            q = i * 4 * step + s
-
-            @pl.when(q != me)
-            def _():
-                pltpu.make_async_remote_copy(
-                    src_ref=outgoing.at[q],
-                    dst_ref=received.at[pl.ds(pl.multiple_of(q * rank, rank), rank)],
-                    send_sem=send1.at[q],
-                    recv_sem=recv1.at[q],
-                    device_id=(q,),
-                    device_id_type=MESH,
-                ).wait_recv()
-
         acc = total[...]
         for s in range(step):
             g = i * step + s
@@ -384,42 +411,45 @@
 
     back_sum[n] = jnp.zeros((rank, rhs), F32)
 
-    def returned(q, carry):
-        @pl.when(q != me)
+    def arrived(i, count):
+        return pltpu.make_async_remote_copy(
+            src_ref=back.at[pl.ds(0, count)],
+            dst_ref=back.at[pl.ds(0, count)],
+            send_sem=send2,
+            recv_sem=recv2.at[i],
+            device_id=(lax.rem(me + 1, n),),
+            device_id_type=MESH,
+        )
+
+    def returned(i, carry):
+        @pl.when(me // part == i)
         def _():
-            pltpu.make_async_remote_copy(
-                src_ref=sums.at[q],
-                dst_ref=back.at[q],
-                send_sem=send2.at[q],
-                recv_sem=recv2.at[q],
-                device_id=(q,),
-                device_id_type=MESH,
-            ).wait_recv()
-
-        back_sum[q] = back[q].astype(F32) + back_sum[prev_ref[qprev + q]]
-        return carry
-
-    lax.fori_loop(0, n, returned, 0, unroll=4)
+            arrived(i, part - 1).wait_recv()
+
+        @pl.when(me // part != i)
+        def _():
+            arrived(i, part).wait_recv()
+
+        for s in range(part):
+            q = i * part + s
+            back_sum[q] = back[q].astype(F32) + back_sum[at(prev_s, qprev + q)]
+        return carry
+
+    lax.fori_loop(0, n // part, returned, 0)
+    arrived(0, n - 1).wait_send()
+
+    def store(g):
+        return pltpu.make_async_copy(out.at[g], out_hbm.at[g], load_sem.at[6 + g])
 
     for g in range(leaves):
-        y = back_sum[last_ref[qlast + g]]
+        y = back_sum[at(last_s, qlast + g)]
         turned = jnp.concatenate([y, pltpu.roll(y, rank, 1)], axis=0).T
         far_f[g, pl.ds(0, half, stride=2), :] = total[g * rank : g * rank + half, :]
         far_f[g, pl.ds(1, half, stride=2), :] = total[g * rank + half : (g + 1) * rank, :]
         far = (far_f[g] + turned[:rank]).astype(BF16)
         down = jnp.dot(basis_t[g], far, preferred_element_type=F32)
-        out[g * leaf : (g + 1) * leaf, :] = (down + near_sum[g]).astype(BF16)
-
-    store = pltpu.make_async_copy(out, out_hbm, load_sem.at[0])
-    store.start()
-
-    def drain(i, carry):
-        q = lax.rem(me + i, n)
-        forward_copy(q).wait_send()
-        back_copy(q).wait_send()
-        return carry
-
-    lax.fori_loop(1, n, drain, 0)
+        out[g] = (down + near_sum[g]).astype(BF16)
+        store(g).start()
 
     @pl.when(has_next)
     def _():
@@ -431,7 +461,8 @@
         to_prior.wait_send()
         rim_prior.wait_send()
 
-    store.wait()
+    for g in range(leaves):
+        store(g).wait()
 
 
 def per_device(
@@ -450,14 +481,17 @@
     rhs = features.shape[1]
     cb, nb = couple_blocks.shape[0], near_blocks.shape[0]
     send = send_list.reshape(-1)
-    prev, last = chains(
+    base = -(-n * leaves // 128) * 128
+    keys = jnp.concatenate(
         [
-            (couple_cols * leaves + couple_rows, n * leaves),
-            (near_rows, leaves),
-            (near_cols, leaves + 2 * HALO),
-            (send, leaves),
+            couple_cols * leaves + couple_rows,
+            near_rows + base,
+            near_cols + (base + leaves),
+            send + (base + 2 * leaves + 2 * HALO),
         ]
     )
+    keys = jnp.pad(keys, (0, -keys.shape[0] % 128), constant_values=-1).reshape(-1, 128)
+    key_rows = keys.shape[0]
     half = rank // 2
     wide = leaves + 2 * HALO
     dma = pltpu.SemaphoreType.DMA
@@ -465,8 +499,8 @@
     anywhere = pl.BlockSpec(memory_space=pl.ANY)
     return pl.pallas_call(
         functools.partial(kernel, n, leaves, rank, leaf, rhs, cb, nb),
-        out_shape=jax.ShapeDtypeStruct(features.shape, BF16),
-        in_specs=[smem] * 5 + [anywhere] * 4,
+        out_shape=jax.ShapeDtypeStruct((leaves, leaf, rhs), BF16),
+        in_specs=[smem, pl.BlockSpec(memory_space=pltpu.VMEM)] + [anywhere] * 4,
         out_specs=anywhere,
         scratch_shapes=[
             pltpu.VMEM((wide, leaf, rhs), BF16),
@@ -493,13 +527,17 @@
             pltpu.VMEM((leaves, leaf, rhs), F32),
             pltpu.VMEM((2, HALO, leaf, rhs), BF16),
             pltpu.VMEM((2, HALO, leaf, rhs), BF16),
-            pltpu.VMEM((leaves * leaf, rhs), BF16),
+            pltpu.VMEM((leaves, leaf, rhs), BF16),
             pltpu.VMEM((leaves, rank, rhs), F32),
-            dma((4,)),
-            dma((n,)),
-            dma((n,)),
-            dma((n,)),
-            dma((n,)),
+            pltpu.VMEM((key_rows, 128), jnp.int32),
+            pltpu.VMEM((base // 128 + 1, 128), jnp.int32),
+            pltpu.SMEM((key_rows, 128), jnp.int32),
+            pltpu.SMEM((base // 128 + 1, 128), jnp.int32),
+            dma((6 + leaves,)),
+            dma,
+            dma,
+            dma,
+            dma((n // min(16, n // 2),)),
             dma((2,)),
             dma((2,)),
             dma((2,)),
@@ -509,16 +547,13 @@
             collective_id=0, has_side_effects=True, vmem_limit_bytes=60 * 1024 * 1024
         ),
     )(
-        send,
-        near_rows,
-        near_cols,
-        prev,
-        last,
+        keys,
+        keys,
         features.reshape(leaves, leaf, rhs),
         basis_t,
         couple_blocks,
         near_blocks,
-    )
+    ).reshape(features.shape)
 
 
 def solution(mesh):

time: 84 us -> 70.4 us (0.84)
  the two profiles are of different devices: /device:TPU:98 before, /device:TPU:34 now
where the time goes in v2:
time: 70.4 us; the launch traced here: 70.1 us
  Pallas kernels  65.5 us (93%)
  other arithmetic  2.7 us (4%)
  local copies, waits for them, and re-layouts  1.87 us (3%)
    pallas_call x1, Pallas kernels, per_device(): pl.pallas_call(functools.partial(kernel, n, leaves, rank, leaf, rhs, cb,...  65.5 us
    unnamed x1, local copies, waits for them, and re-layouts  1.87 us

profile of v2, /device:TPU:34, one launch (start us, length us, event | category | flops | bytes accessed | tf_op | source)
XLA Modules:
  0.0 70.1 jit_solution(5361625218259145504)
XLA Ops:
  0.0 0.7 add_bitcast_fusion.1
  0.7 0.7 broadcast_add_fusion
  1.3 0.7 multiply_add_fusion
  2.0 0.7 add_bitcast_fusion.key_ref.keys
  2.7 65.5 %shard_map.91 = bf16[8,256,128]{2,1,0:T(8,128)(2,1)} custom-call(s32[5,128]{1,0:T(8,128)} %add_bitcast_fusion.key_ref.keys, s32[5,128]{1,0:T(8,128)} %add_bitcast_fusion.key_ref.keys, bf16[8,256,128]{2,1,0:T(8,128)(2,1)} %bitcast.7, bf16[8,64,256]{2,1,0:T(8,128)(2,1)} %basis_hbm.1, bf16[384,4096]{1,0:T(8,128)(2,1)} %blocks_hbm.1, bf16[64,256,256]{2,1,0:T(8,128)(2,1)} %near_hbm.1), custom_call_target="tpu_custom_call" | custom-call | tf_op jit(solution)/shard_map/pallas_call | solution.py:500
  68.3 1.9 %copy.11 = bf16[2048,128]{1,0:T(8,128)(2,1)} copy(bf16[2048,128]{1,0:T(8,128)(2,1)} %bitcast.6) | data formatting | bytes 1048576

commit v3 on v2

--- a/solution.py
+++ b/solution.py
@@ -46,6 +46,14 @@
         last_ref[b : b + 1, :] = settle(found, lane + b * 128, [(first, parts[part]) for first, part in id_parts])
 
 
+def pass_on(src, dst, sems):
+    copies = [pltpu.make_async_copy(src.at[g], dst.at[g], sems.at[g]) for g in range(src.shape[0])]
+    for copy in copies:
+        copy.start()
+    for copy in copies:
+        copy.wait()
+
+
 def near_first(n):
     steps = [(o // 32, o // 8 % 4, o // 2 % 4, o % 2) for o in range(1, n)]
     random.Random(0).shuffle(steps)
@@ -61,8 +69,14 @@
     rhs,
     cb,
     nb,
-    key_ref,
-    keys,
+    send_ref,
+    nrows_ref,
+    ncols_ref,
+    rows_v,
+    cols_v,
+    nrows_v,
+    ncols_v,
+    send_v,
     x_hbm,
     basis_hbm,
     blocks_hbm,
@@ -94,6 +108,7 @@
     rim_in,
     out,
     far_f,
+    keys,
     prev_v,
     last_v,
     prev_s,
@@ -110,7 +125,8 @@
 ):
     me = lax.axis_index("clus")
     base = last_v.shape[0] * 128 - 128
-    rprev, kprev, qprev = cb, cb + nb, cb + 2 * nb
+    rprev = rows_v.shape[0] * 128
+    kprev, qprev = rprev + 128, rprev + 256
     rlast, klast, qlast = base, base + leaves, base + 2 * leaves + 2 * HALO
     parts = [(0, cb), (rprev, nb), (kprev, nb), (qprev, n)]
     id_parts = [(0, 0), (rlast, 1), (klast, 2), (qlast, 3)]
@@ -119,7 +135,7 @@
         return ref[i // 128, i % 128]
 
     def target(q):
-        return jnp.maximum(at(key_ref, qprev + q) - qlast, 0)
+        return send_ref[q]
 
     half = rank // 2
     lane = lax.broadcasted_iota(jnp.int32, (rank, 2 * rank), 1)
@@ -134,7 +150,6 @@
     load_n = pltpu.make_async_copy(near_hbm, near, load_sem.at[3])
     load_x.start()
     load_b.start()
-    load_s.start()
 
     def greet(i, carry):
         q = lax.rem(me + i, n)
@@ -145,6 +160,7 @@
 
     load_x.wait()
     load_b.wait()
+    load_s.start()
 
     def coefficients(g, carry):
         c = jnp.dot(basis[g], xext[HALO + g], preferred_element_type=F32).astype(BF16)
@@ -221,6 +237,13 @@
         tile = jnp.concatenate(rows, axis=0)
         coef_t[:, pair * 2 * rank : (pair + 1) * 2 * rank] = tile.T.astype(BF16)
 
+    keys[...] = jnp.full(keys.shape, -1, jnp.int32)
+    for b in range(rows_v.shape[0]):
+        keys[b : b + 1, :] = cols_v[b : b + 1, :] * leaves + rows_v[b : b + 1, :]
+    b = rows_v.shape[0]
+    keys[b : b + 1, 0:nb] = nrows_v[...] + rlast
+    keys[b + 1 : b + 2, 0:nb] = ncols_v[...] + klast
+    keys[b + 2 : b + 3, 0:n] = send_v[...] + qlast
     chains(keys, prev_v, last_v, parts, id_parts)
     prev_load = pltpu.make_async_copy(prev_v, prev_s, load_sem.at[4])
     last_load = pltpu.make_async_copy(last_v, last_s, load_sem.at[5])
@@ -315,7 +338,7 @@
     work[nb] = jnp.zeros((leaf, rhs), F32)
 
     def near_rows(k, carry):
-        y = jnp.dot(near[k], xext[jnp.maximum(at(key_ref, kprev + k) - klast, 0)], preferred_element_type=F32)
+        y = jnp.dot(near[k], xext[ncols_ref[k]], preferred_element_type=F32)
         work[k] = y + work[at(prev_s, rprev + k)]
         return carry
 
@@ -324,7 +347,7 @@
         near_sum[g] = work[at(last_s, rlast + g)]
 
     def near_cols(k, carry):
-        y = jnp.dot(x_t[jnp.maximum(at(key_ref, rprev + k) - rlast, 0)], near[k], preferred_element_type=F32)
+        y = jnp.dot(x_t[nrows_ref[k]], near[k], preferred_element_type=F32)
         before = work[at(prev_s, kprev + k)]
         for h in range(2):
             rows = slice(h * rhs, (h + 1) * rhs)
@@ -482,25 +505,16 @@
     cb, nb = couple_blocks.shape[0], near_blocks.shape[0]
     send = send_list.reshape(-1)
     base = -(-n * leaves // 128) * 128
-    keys = jnp.concatenate(
-        [
-            couple_cols * leaves + couple_rows,
-            near_rows + base,
-            near_cols + (base + leaves),
-            send + (base + 2 * leaves + 2 * HALO),
-        ]
-    )
-    keys = jnp.pad(keys, (0, -keys.shape[0] % 128), constant_values=-1).reshape(-1, 128)
-    key_rows = keys.shape[0]
+    key_rows = cb // 128 + 3
     half = rank // 2
     wide = leaves + 2 * HALO
     dma = pltpu.SemaphoreType.DMA
     smem = pl.BlockSpec(memory_space=pltpu.SMEM)
     anywhere = pl.BlockSpec(memory_space=pl.ANY)
-    return pl.pallas_call(
+    result = pl.pallas_call(
         functools.partial(kernel, n, leaves, rank, leaf, rhs, cb, nb),
         out_shape=jax.ShapeDtypeStruct((leaves, leaf, rhs), BF16),
-        in_specs=[smem, pl.BlockSpec(memory_space=pltpu.VMEM)] + [anywhere] * 4,
+        in_specs=[smem] * 3 + [pl.BlockSpec(memory_space=pltpu.VMEM)] * 5 + [anywhere] * 4,
         out_specs=anywhere,
         scratch_shapes=[
             pltpu.VMEM((wide, leaf, rhs), BF16),
@@ -530,6 +544,7 @@
             pltpu.VMEM((leaves, leaf, rhs), BF16),
             pltpu.VMEM((leaves, rank, rhs), F32),
             pltpu.VMEM((key_rows, 128), jnp.int32),
+            pltpu.VMEM((key_rows, 128), jnp.int32),
             pltpu.VMEM((base // 128 + 1, 128), jnp.int32),
             pltpu.SMEM((key_rows, 128), jnp.int32),
             pltpu.SMEM((base // 128 + 1, 128), jnp.int32),
@@ -547,13 +562,26 @@
             collective_id=0, has_side_effects=True, vmem_limit_bytes=60 * 1024 * 1024
         ),
     )(
-        keys,
-        keys,
+        send,
+        near_rows,
+        near_cols,
+        couple_rows.reshape(-1, 128),
+        couple_cols.reshape(-1, 128),
+        near_rows.reshape(1, nb),
+        near_cols.reshape(1, nb),
+        send.reshape(1, n),
         features.reshape(leaves, leaf, rhs),
         basis_t,
         couple_blocks,
         near_blocks,
-    ).reshape(features.shape)
+    )
+    return pl.pallas_call(
+        pass_on,
+        out_shape=jax.ShapeDtypeStruct(result.shape, BF16),
+        in_specs=[anywhere],
+        out_specs=anywhere,
+        scratch_shapes=[dma((leaves,))],
+    )(result).reshape(features.shape)
 
 
 def solution(mesh):

time: 70.4 us -> 83 us (1.18)
  Pallas kernels: 65.5 us -> 82.9 us
  other arithmetic: 2.7 us -> 0 us
  local copies, waits for them, and re-layouts: 1.87 us -> 0 us
    pallas_call x0 -> x1, Pallas kernels: none -> 17.1 us  [per_device(): pl.pallas_call(pass_on, out_shape=jax.ShapeDtypeStruct(result.shape, BF16...]
    add x3 -> x0, other arithmetic: 2.03 us -> none  [the longest x1 0.7 us: per_device(): couple_cols * leaves + couple_rows]
    unnamed x1 -> x0, local copies, waits for them, and re-layouts: 1.87 us -> none
where the time goes in v3:
time: 83 us; the launch traced here: 82.9 us
  Pallas kernels  82.9 us (100%)
    pallas_call x1, Pallas kernels, per_device(): pl.pallas_call(functools.partial(kernel, n, leaves, rank, leaf, rhs, cb,...  65.8 us
    pallas_call x1, Pallas kernels, per_device(): pl.pallas_call(pass_on, out_shape=jax.ShapeDtypeStruct(result.shape, BF16...  17.1 us

profile of v3, /device:TPU:34, one launch (start us, length us, event | category | flops | bytes accessed | tf_op | source)
XLA Modules:
  0.0 82.9 jit_solution(13052614695236913900)
XLA Ops:
  0.0 65.8 %shard_map.91.src = bf16[8,256,128]{2,1,0:T(8,128)(2,1)} custom-call(s32[128]{0:T(128)} %bitcast.11, s32[64]{0:T(128)} %nrows_ref.1, s32[64]{0:T(128)} %ncols_ref.1, s32[3,128]{1,0:T(4,128)} %bitcast.9, s32[3,128]{1,0:T(4,128)} %bitcast.10, s32[1,64]{1,0:T(1,128)} %bitcast.13, s32[1,64]{1,0:T(1,128)} %bitcast.14, s32[1,128]{1,0:T(1,128)} %bitcast.12, ...), custom_call_target="tpu_custom_call" | custom-call | tf_op jit(solution)/shard_map/pallas_call | solution.py:514
  65.8 17.1 %shard_map.92 = bf16[8,256,128]{2,1,0:T(8,128)(2,1)} custom-call(bf16[8,256,128]{2,1,0:T(8,128)(2,1)} %shard_map.91.src), custom_call_target="tpu_custom_call" | custom-call | tf_op jit(solution)/shard_map/pallas_call | solution.py:578

commit v4 on v3

--- a/solution.py
+++ b/solution.py
@@ -44,14 +44,6 @@
             best = jnp.where(down[other] == lane + b * 128, row + other * 128, best)
         found = jnp.max(best, axis=0, keepdims=True)
         last_ref[b : b + 1, :] = settle(found, lane + b * 128, [(first, parts[part]) for first, part in id_parts])
-
-
-def pass_on(src, dst, sems):
-    copies = [pltpu.make_async_copy(src.at[g], dst.at[g], sems.at[g]) for g in range(src.shape[0])]
-    for copy in copies:
-        copy.start()
-    for copy in copies:
-        copy.wait()
 
 
 def near_first(n):
@@ -511,7 +503,7 @@
     dma = pltpu.SemaphoreType.DMA
     smem = pl.BlockSpec(memory_space=pltpu.SMEM)
     anywhere = pl.BlockSpec(memory_space=pl.ANY)
-    result = pl.pallas_call(
+    return pl.pallas_call(
         functools.partial(kernel, n, leaves, rank, leaf, rhs, cb, nb),
         out_shape=jax.ShapeDtypeStruct((leaves, leaf, rhs), BF16),
         in_specs=[smem] * 3 + [pl.BlockSpec(memory_space=pltpu.VMEM)] * 5 + [anywhere] * 4,
@@ -574,14 +566,7 @@
         basis_t,
         couple_blocks,
         near_blocks,
-    )
-    return pl.pallas_call(
-        pass_on,
-        out_shape=jax.ShapeDtypeStruct(result.shape, BF16),
-        in_specs=[anywhere],
-        out_specs=anywhere,
-        scratch_shapes=[dma((leaves,))],
-    )(result).reshape(features.shape)
+    ).reshape(features.shape)
 
 
 def solution(mesh):

time: 83 us -> 67.9 us (0.82)
  Pallas kernels: 82.9 us -> 65.8 us
  local copies, waits for them, and re-layouts: 0 us -> 1.87 us
    pallas_call x1 -> x0, Pallas kernels: 17.1 us -> none  [per_device(): pl.pallas_call(pass_on, out_shape=jax.ShapeDtypeStruct(result.shape, BF16...]
    unnamed x0 -> x1, local copies, waits for them, and re-layouts: none -> 1.87 us
where the time goes in v4:
time: 67.9 us; the launch traced here: 67.7 us
  Pallas kernels  65.8 us (97%)
  local copies, waits for them, and re-layouts  1.87 us (3%)
    pallas_call x1, Pallas kernels, per_device(): pl.pallas_call(functools.partial(kernel, n, leaves, rank, leaf, rhs, cb,...  65.8 us
    unnamed x1, local copies, waits for them, and re-layouts  1.87 us

profile of v4, /device:TPU:34, one launch (start us, length us, event | category | flops | bytes accessed | tf_op | source)
XLA Modules:
  0.0 67.7 jit_solution(15500345422819264902)
XLA Ops:
  0.0 65.8 %shard_map.91 = bf16[8,256,128]{2,1,0:T(8,128)(2,1)} custom-call(s32[128]{0:T(128)} %bitcast.12, s32[64]{0:T(128)} %nrows_ref.1, s32[64]{0:T(128)} %ncols_ref.1, s32[3,128]{1,0:T(4,128)} %bitcast.10, s32[3,128]{1,0:T(4,128)} %bitcast.11, s32[1,64]{1,0:T(1,128)} %bitcast.14, s32[1,64]{1,0:T(1,128)} %bitcast.15, s32[1,128]{1,0:T(1,128)} %bitcast.13, ...), custom_call_target="tpu_custom_call" | custom-call | tf_op jit(solution)/shard_map/pallas_call | solution.py:506
  65.8 1.9 %copy.11 = bf16[2048,128]{1,0:T(8,128)(2,1)} copy(bf16[2048,128]{1,0:T(8,128)(2,1)} %bitcast.8) | data formatting | bytes 1048576

commit v5 on v4

--- a/solution.py
+++ b/solution.py
@@ -279,7 +279,7 @@
         )
 
     def mirror(i, carry):
-        g = lax.rem(my_group + i * 13, groups)
+        g = lax.rem(my_group + i * 5, groups)
         rows = []
         for r in range(leaves):
             upper, lower = [], []

time: 67.9 us -> 67.1 us (0.988); the launches traced: 67.7 us -> 65.9 us
  Pallas kernels: 65.8 us -> 64 us
    pallas_call x1, Pallas kernels: 65.8 us -> 64 us  [per_device(): pl.pallas_call(functools.partial(kernel, n, leaves, rank, leaf, rhs, cb,...]
where the time goes in v5:
time: 67.1 us; the launch traced here: 65.9 us
  Pallas kernels  64 us (95%)
  local copies, waits for them, and re-layouts  1.87 us (3%)
    pallas_call x1, Pallas kernels, per_device(): pl.pallas_call(functools.partial(kernel, n, leaves, rank, leaf, rhs, cb,...  64 us
    unnamed x1, local copies, waits for them, and re-layouts  1.87 us

profile of v5, /device:TPU:34, one launch (start us, length us, event | category | flops | bytes accessed | tf_op | source)
XLA Modules:
  0.0 65.9 jit_solution(10925303205452481836)
XLA Ops:
  0.0 64.0 %shard_map.91 = bf16[8,256,128]{2,1,0:T(8,128)(2,1)} custom-call(s32[128]{0:T(128)} %bitcast.12, s32[64]{0:T(128)} %nrows_ref.1, s32[64]{0:T(128)} %ncols_ref.1, s32[3,128]{1,0:T(4,128)} %bitcast.10, s32[3,128]{1,0:T(4,128)} %bitcast.11, s32[1,64]{1,0:T(1,128)} %bitcast.14, s32[1,64]{1,0:T(1,128)} %bitcast.15, s32[1,128]{1,0:T(1,128)} %bitcast.13, ...), custom_call_target="tpu_custom_call" | custom-call | tf_op jit(solution)/shard_map/pallas_call | solution.py:506
  64.0 1.9 %copy.11 = bf16[2048,128]{1,0:T(8,128)(2,1)} copy(bf16[2048,128]{1,0:T(8,128)(2,1)} %bitcast.8) | data formatting | bytes 1048576

commit v6 on v5

--- a/solution.py
+++ b/solution.py
@@ -411,6 +411,9 @@
         return carry
 
     lax.fori_loop(0, groups // step, forward, 0)
+    for g in range(leaves):
+        far_f[g, pl.ds(0, half, stride=2), :] = total[g * rank : g * rank + half, :]
+        far_f[g, pl.ds(1, half, stride=2), :] = total[g * rank + half : (g + 1) * rank, :]
 
     @pl.when(has_next)
     def _():
@@ -451,7 +454,6 @@
         return carry
 
     lax.fori_loop(0, n // part, returned, 0)
-    arrived(0, n - 1).wait_send()
 
     def store(g):
         return pltpu.make_async_copy(out.at[g], out_hbm.at[g], load_sem.at[6 + g])
@@ -459,8 +461,6 @@
     for g in range(leaves):
         y = back_sum[at(last_s, qlast + g)]
         turned = jnp.concatenate([y, pltpu.roll(y, rank, 1)], axis=0).T
-        far_f[g, pl.ds(0, half, stride=2), :] = total[g * rank : g * rank + half, :]
-        far_f[g, pl.ds(1, half, stride=2), :] = total[g * rank + half : (g + 1) * rank, :]
         far = (far_f[g] + turned[:rank]).astype(BF16)
         down = jnp.dot(basis_t[g], far, preferred_element_type=F32)
         out[g] = (down + near_sum[g]).astype(BF16)
@@ -476,6 +476,7 @@
         to_prior.wait_send()
         rim_prior.wait_send()
 
+    arrived(0, n - 1).wait_send()
     for g in range(leaves):
         store(g).wait()
 

time: 67.1 us -> 67.1 us (level)
  no operation moved by 1% of the time
where the time goes in v6:
time: 67.1 us; the launch traced here: 65.9 us
  Pallas kernels  64 us (95%)
  local copies, waits for them, and re-layouts  1.87 us (3%)
    pallas_call x1, Pallas kernels, per_device(): pl.pallas_call(functools.partial(kernel, n, leaves, rank, leaf, rhs, cb,...  64 us
    unnamed x1, local copies, waits for them, and re-layouts  1.87 us

profile of v6, /device:TPU:34, one launch (start us, length us, event | category | flops | bytes accessed | tf_op | source)
XLA Modules:
  0.0 65.9 jit_solution(2840622431840548538)
XLA Ops:
  0.0 64.0 %shard_map.91 = bf16[8,256,128]{2,1,0:T(8,128)(2,1)} custom-call(s32[128]{0:T(128)} %bitcast.12, s32[64]{0:T(128)} %nrows_ref.1, s32[64]{0:T(128)} %ncols_ref.1, s32[3,128]{1,0:T(4,128)} %bitcast.10, s32[3,128]{1,0:T(4,128)} %bitcast.11, s32[1,64]{1,0:T(1,128)} %bitcast.14, s32[1,64]{1,0:T(1,128)} %bitcast.15, s32[1,128]{1,0:T(1,128)} %bitcast.13, ...), custom_call_target="tpu_custom_call" | custom-call | tf_op jit(solution)/shard_map/pallas_call | solution.py:507
  64.0 1.9 %copy.11 = bf16[2048,128]{1,0:T(8,128)(2,1)} copy(bf16[2048,128]{1,0:T(8,128)(2,1)} %bitcast.8) | data formatting | bytes 1048576

commit v7 on v5

--- a/solution.py
+++ b/solution.py
@@ -180,12 +180,6 @@
         dx, dz, dy, dc = step
         return (((x + dx) % (n // 32) * 4 + (z + dz) % 4) * 4 + (y + dy) % 4) * 2 + (core + dc) % 2
 
-    for step in near_first(n):
-        q = peer(step)
-        outgoing[q] = coef[target(q)]
-        forward_copy(q).start()
-    received[pl.ds(pl.multiple_of(me * rank, rank), rank), :] = coef[target(me)]
-
     to_next = pltpu.make_async_remote_copy(
         src_ref=xext.at[pl.ds(leaves, HALO)],
         dst_ref=xext.at[pl.ds(0, HALO)],
@@ -212,6 +206,12 @@
     @pl.when(has_prior)
     def _():
         to_prior.start()
+
+    for step in near_first(n):
+        q = peer(step)
+        outgoing[q] = coef[target(q)]
+        forward_copy(q).start()
+    received[pl.ds(pl.multiple_of(me * rank, rank), rank), :] = coef[target(me)]
 
     @pl.when(jnp.logical_not(has_prior))
     def _():

time: 67.1 us -> 69.1 us (1.030)
  the two profiles are of different devices: /device:TPU:34 before, /device:TPU:1 now
where the time goes in v7:
time: 69.1 us; the launch traced here: 69 us
  Pallas kernels  67.1 us (97%)
  local copies, waits for them, and re-layouts  1.87 us (3%)
    pallas_call x1, Pallas kernels, per_device(): pl.pallas_call(functools.partial(kernel, n, leaves, rank, leaf, rhs, cb,...  67.1 us
    unnamed x1, local copies, waits for them, and re-layouts  1.87 us

profile of v7, /device:TPU:1, one launch (start us, length us, event | category | flops | bytes accessed | tf_op | source)
XLA Modules:
  0.0 69.0 jit_solution(7666738659777857224)
XLA Ops:
  0.0 67.1 %shard_map.91 = bf16[8,256,128]{2,1,0:T(8,128)(2,1)} custom-call(s32[128]{0:T(128)} %bitcast.12, s32[64]{0:T(128)} %nrows_ref.1, s32[64]{0:T(128)} %ncols_ref.1, s32[3,128]{1,0:T(4,128)} %bitcast.10, s32[3,128]{1,0:T(4,128)} %bitcast.11, s32[1,64]{1,0:T(1,128)} %bitcast.14, s32[1,64]{1,0:T(1,128)} %bitcast.15, s32[1,128]{1,0:T(1,128)} %bitcast.13, ...), custom_call_target="tpu_custom_call" | custom-call | tf_op jit(solution)/shard_map/pallas_call | solution.py:506
  67.1 1.9 %copy.11 = bf16[2048,128]{1,0:T(8,128)(2,1)} copy(bf16[2048,128]{1,0:T(8,128)(2,1)} %bitcast.8) | data formatting | bytes 1048576
